TPU v7x, 256 devices: a whole 4x4x8 slice. The times are simulated.
256 devices in a mesh: row: 16 (over y, x), col: 16 (over z, core).
Axes of the slice: x: 4, y: 4, z: 8, core: 2. Of those that a mesh axis runs over, the one named last changes fastest.
Arguments:
- slab: float32 [32768, 16384], P('row', 'col'), may hold values from -30 to 30, as said below
- test_matrix: float32 [16384, 128], P('col'), may hold values from -0.046875 to 0.046875
Outputs:
- basis: float32 [32768, 128], P(('row', 'col'))
- r_factor: float32 [128, 128], replicated
Inputs may be any that keep to these rules, and one draw needn't show every extreme that they name: `slab`: the sketch's condition number (largest over smallest singular value) is at most 2000.
All inputs are finite; a program needn't handle non-finite values.
Results may differ from a plain program's by a relative error of at most 0.0003.
Values sent between devices are 32-bit elements; how exact they have to be, the bound alone decides.
No kernel may reach another device: no remote copies, remote signals or barrier semaphores. Data moves between devices by JAX's collectives and lax.ppermute only.
A program may use at most 64 MiB of HBM per device.

v0:
```python
import math
import jax
import jax.numpy as jnp
from jax import lax
from jax.sharding import PartitionSpec as P

HIGHEST = lax.Precision.HIGHEST
CONTRACT = (((0,), (0,)), ((), ()))


def gram_of(matrix):
    return lax.dot_general(
        matrix, matrix, CONTRACT, precision=HIGHEST, preferred_element_type=jnp.float32
    )


def orthonormal(matrix, summed):
    lower_one = jnp.linalg.cholesky(summed(gram_of(matrix)))
    inner = lax.linalg.triangular_solve(
        lower_one, matrix, left_side=False, lower=True, transpose_a=True
    )
    lower_two = jnp.linalg.cholesky(summed(gram_of(inner)))
    result = lax.linalg.triangular_solve(
        lower_two, inner, left_side=False, lower=True, transpose_a=True
    )
    factor = jnp.dot(
        lower_two.T, lower_one.T, precision=HIGHEST, preferred_element_type=jnp.float32
    )
    return (result, factor)


def sum_everywhere(gram):
    return lax.psum(gram, ("row", "col"))


def local(slab, test_matrix):
    row_total = slab.shape[0] * lax.axis_size("row")
    root_rows = math.sqrt(row_total)
    partial_value = jnp.dot(
        slab, test_matrix, precision=HIGHEST, preferred_element_type=jnp.float32
    )
    sketch_one = lax.psum(partial_value, "col")
    pulled_part = lax.dot_general(
        slab, sketch_one, CONTRACT, precision=HIGHEST, preferred_element_type=jnp.float32
    )
    pulled = lax.psum(pulled_part, "row") / row_total
    owned = lax.psum_scatter(
        jnp.dot(slab, pulled, precision=HIGHEST, preferred_element_type=jnp.float32),
        "col",
        scatter_dimension=0,
        tiled=True,
    )
    result, factor = orthonormal(owned, sum_everywhere)
    return (result * root_rows, factor / root_rows)


def solution(mesh):
    in_specs = (P("row", "col"), P("col", None))
    out_specs = (P(("row", "col"), None), P())
    return jax.shard_map(local, mesh=mesh, in_specs=in_specs, out_specs=out_specs, check_vma=False)
```

profile of v0, /device:TPU:1, one launch (start us, length us, event | category | flops | bytes accessed | tf_op | source)
XLA Modules:
  0.0 847.2 jit_solution(4430770114689326085)
XLA Ops:
  7.2 0.0 copy-start
  7.2 0.0 all-reduce.5.cloned.1.call-start
  7.2 1.0 copy-done
  8.2 9.8 %fusion.22 = f32[2048,128]{1,0:T(8,128)} fusion(f32[2048,1024]{1,0:T(8,128)} %param.5, f32[1024,128]{1,0:T(8,128)S(1)} %copy-done), kind=kOutput, calls=%fused_computation.33 | convolution fusion | flops 3221225472 | bytes 9961472 | tf_op jit(solution)/shard_map/dot_general | solution.py:39
  18.1 0.0 all-reduce.5.cloned.1.call-update
  18.1 0.0 all-reduce.7.cloned.1.call-start
  18.1 115.1 %all-reduce.5.cloned.1.call-done = f32[2048,128]{1,0:T(8,128)} async-done(((f32[2048,128]{1,0:T(8,128)}), f32[2048,128]{1,0:T(8,128)}) %all-reduce.5.cloned.1.call-update) | async-done | bytes 1048592 | tf_op jit(solution)/shard_map/psum | solution.py:42
  133.2 9.2 %convolution_bitcast_fusion.1 = f32[1024,128]{0,1:T(8,128)} fusion(f32[2048,128]{1,0:T(8,128)} %all-reduce.5.cloned.1.call-done, f32[2048,1024]{1,0:T(8,128)} %param.5), kind=kOutput, calls=%fused_computation.1 | convolution fusion | flops 3221225472 | bytes 9961472 | tf_op jit(solution)/shard_map/dot_general | solution.py:43
  142.4 0.0 all-reduce.7.cloned.1.call-update
  142.4 0.2 reduce-scatter.2.cloned.1.call-start
  142.7 94.3 %all-reduce.7.cloned.1.call-done = f32[1024,128]{0,1:T(8,128)} async-done(((f32[1024,128]{0,1:T(8,128)}), f32[1024,128]{0,1:T(8,128)}) %all-reduce.7.cloned.1.call-update) | async-done | bytes 524304 | tf_op jit(solution)/shard_map/psum | solution.py:46
  236.9 13.0 %convolution_bitcast_fusion = f32[2048,128]{0,1:T(8,128)} fusion(f32[2048,1024]{1,0:T(8,128)} %param.5, f32[1024,128]{0,1:T(8,128)} %all-reduce.7.cloned.1.call-done), kind=kOutput, calls=%fused_computation | convolution fusion | flops 3221356544 | bytes 9961472 | tf_op jit(solution)/shard_map/dot_general | solution.py:48
  249.9 0.0 reduce-scatter.2.cloned.1.call-update
  249.9 0.0 all-reduce.9.cloned.1.call-start
  250.0 55.4 %reduce-scatter.2.cloned.1.call-done = f32[128,128]{0,1:T(8,128)} async-done(((f32[2048,128]{0,1:T(8,128)}), f32[128,128]{0,1:T(8,128)}) %reduce-scatter.2.cloned.1.call-update) | async-done | bytes 65552 | tf_op jit(solution)/shard_map/reduce_scatter | solution.py:47
  305.3 1.8 fusion.23
  307.1 0.0 all-reduce.9.cloned.1.call-update
  307.2 0.3 all-reduce.11.cloned.1.call-start
  307.4 244.3 %all-reduce.9.cloned.1.call-done = f32[128,128]{0,1:T(8,128)} async-done(((f32[128,128]{0,1:T(8,128)}), f32[128,128]{0,1:T(8,128)}) %all-reduce.9.cloned.1.call-update) | async-done | bytes 65552 | tf_op jit(solution)/shard_map/psum | solution.py:33
  551.7 0.9 copy.5
  552.7 0.9 fusion.6
  553.5 11.7 %cholesky.44 = f32[128,128]{1,0:T(8,128)S(1)} custom-call(f32[128,128]{1,0:T(8,128)S(1)} %fusion.6), custom_call_target="Cholesky" | custom-call | tf_op jit(solution)/shard_map/jit(cholesky)/cholesky | solution.py:18
  565.3 0.6 compare_reduce_fusion.1
  565.9 0.7 fusion.10
  566.6 9.8 %custom-call.6 = f32[1,128,128]{1,2,0:T(8,128)S(1)} custom-call(f32[1,128,128]{2,1,0:T(8,128)S(1)} %fusion.10), custom_call_target="InvertDiagBlocksLowerTriangular" | custom-call | tf_op jit(solution)/shard_map/triangular_solve/custom-call.0 | solution.py:19
  576.4 1.1 convolution_bitcast_fusion.3
  577.5 0.9 fusion.24
  578.4 0.0 all-reduce.11.cloned.1.call-update
  578.4 234.2 %all-reduce.11.cloned.1.call-done = f32[128,128]{0,1:T(8,128)} async-done(((f32[128,128]{0,1:T(8,128)}), f32[128,128]{0,1:T(8,128)}) %all-reduce.11.cloned.1.call-update) | async-done | bytes 65552 | tf_op jit(solution)/shard_map/psum | solution.py:33
  812.6 0.9 copy.7
  813.5 0.9 fusion.4
  814.4 11.7 %cholesky.55 = f32[128,128]{1,0:T(8,128)S(1)} custom-call(f32[128,128]{1,0:T(8,128)S(1)} %fusion.4), custom_call_target="Cholesky" | custom-call | tf_op jit(solution)/shard_map/jit(cholesky)/cholesky | solution.py:22
  826.1 0.7 compare_reduce_fusion
  826.9 2.3 convolution_multiply_fusion
  829.1 0.7 select_bitcast_fusion
  829.8 9.8 %custom-call.7 = f32[1,128,128]{1,2,0:T(8,128)S(1)} custom-call(f32[1,128,128]{2,1,0:T(8,128)S(1)} %select_bitcast_fusion), custom_call_target="InvertDiagBlocksLowerTriangular" | custom-call | tf_op jit(solution)/shard_map/triangular_solve/custom-call.0 | solution.py:23
  839.6 0.3 fusion
  839.9 0.7 copy.8
  (2 shorter events, 0.1 us)
Async XLA Ops:
  7.2 1.0 copy-start
  7.2 126.1 %all-reduce.5.cloned.1.call-start = ((), (), s32[]{:S(2)}) async-start(), calls=%async_computation.1 | async-start | bytes 2097152 | tf_op jit(solution)/shard_map/psum | solution.py:42
  18.1 218.8 %all-reduce.7.cloned.1.call-start = ((), (), s32[]{:S(2)}) async-start(), calls=%async_computation.2 | async-start | bytes 1048576 | tf_op jit(solution)/shard_map/psum | solution.py:46
  142.4 162.9 %reduce-scatter.2.cloned.1.call-start = ((), (), s32[]{:S(2)}) async-start(), calls=%async_computation.3 | async-start | bytes 1114112 | tf_op jit(solution)/shard_map/reduce_scatter | solution.py:47
  249.9 301.8 %all-reduce.9.cloned.1.call-start = ((), (), s32[]{:S(2)}) async-start(), calls=%async_computation.4 | async-start | bytes 131072 | tf_op jit(solution)/shard_map/psum | solution.py:33
  307.2 505.4 %all-reduce.11.cloned.1.call-start = ((), (), s32[]{:S(2)}) async-start(), calls=%async_computation.5 | async-start | bytes 131072 | tf_op jit(solution)/shard_map/psum | solution.py:33
Sparse Core Ops, SparseCore 0:
  18.2 114.9 all-reduce.4
  142.5 94.3 all-reduce.6
  250.1 55.2 reduce-scatter.1
  312.2 239.4 all-reduce.8
  578.6 234.0 all-reduce.10
where the time goes:
time: 848 us; the launch traced here: 847 us
  waiting for transfers between devices  743 us (88%)
  other arithmetic  47.5 us (6%)
  matrix products  38.4 us (5%)
  between operations  13.9 us (2%)
    psum x2, waiting for transfers between devices, sum_everywhere(): return lax.psum(gram, ('row', 'col'))  478 us
    psum x1, waiting for transfers between devices, local(): sketch_one = lax.psum(partial_value, 'col')  115 us
    psum x1, waiting for transfers between devices, local(): pulled = lax.psum(pulled_part, 'row') / row_total  94.3 us
    reduce_scatter x1, waiting for transfers between devices, local(): lax.psum_scatter(jnp.dot(slab, pulled, precision=HIGHEST, preferred_eleme...  55.4 us
  transfers between devices with their start and end apart: 5, of which 5 were waited for; matrix products, arithmetic and copies ran while one was open for 0% of the time, Pallas kernels for 0%

commit v1 on v0

--- a/solution.py
+++ b/solution.py
@@ -30,7 +30,7 @@
 
 
 def sum_everywhere(gram):
-    return lax.psum(gram, ("row", "col"))
+    return lax.psum(lax.psum(gram, "col"), "row")
 
 
 def local(slab, test_matrix):

time: 848 us -> 753 us (0.89)
  waiting for transfers between devices: 743 us -> 648 us
    psum x2 -> x4, waiting for transfers between devices: 478 us -> 383 us  [sum_everywhere(): return lax.psum(lax.psum(gram, 'col'), 'row')]
  transfers between devices with their start and end apart: 5 -> 7, of which waited for: 5 -> 7; matrix products, arithmetic and copies ran while one was open for 0% -> 0% of each run, Pallas kernels for 0% -> 0%
where the time goes in v1:
time: 753 us; the launch traced here: 752 us
  waiting for transfers between devices  648 us (86%)
  other arithmetic  47.5 us (6%)
  matrix products  38.4 us (5%)
  between operations  14.2 us (2%)
    psum x4, waiting for transfers between devices, sum_everywhere(): return lax.psum(lax.psum(gram, 'col'), 'row')  383 us
    psum x1, waiting for transfers between devices, local(): sketch_one = lax.psum(partial_value, 'col')  115 us
    psum x1, waiting for transfers between devices, local(): pulled = lax.psum(pulled_part, 'row') / row_total  94.3 us
    reduce_scatter x1, waiting for transfers between devices, local(): lax.psum_scatter(jnp.dot(slab, pulled, precision=HIGHEST, preferred_eleme...  55.4 us
  transfers between devices with their start and end apart: 7, of which 7 were waited for; matrix products, arithmetic and copies ran while one was open for 0% of the time, Pallas kernels for 0%

profile of v1, /device:TPU:1, one launch (start us, length us, event | category | flops | bytes accessed | tf_op | source)
XLA Modules:
  0.0 752.5 jit_solution(16067750251647953246)
XLA Ops:
  7.2 0.0 copy-start
  7.2 0.0 all-reduce.7.cloned.1.call-start
  7.2 1.0 copy-done
  8.2 9.8 %fusion.22 = f32[2048,128]{1,0:T(8,128)} fusion(f32[2048,1024]{1,0:T(8,128)} %param.5, f32[1024,128]{1,0:T(8,128)S(1)} %copy-done), kind=kOutput, calls=%fused_computation.33 | convolution fusion | flops 3221225472 | bytes 9961472 | tf_op jit(solution)/shard_map/dot_general | solution.py:39
  18.1 0.0 all-reduce.7.cloned.1.call-update
  18.1 0.0 all-reduce.9.cloned.1.call-start
  18.1 115.1 %all-reduce.7.cloned.1.call-done = f32[2048,128]{1,0:T(8,128)} async-done(((f32[2048,128]{1,0:T(8,128)}), f32[2048,128]{1,0:T(8,128)}) %all-reduce.7.cloned.1.call-update) | async-done | bytes 1048592 | tf_op jit(solution)/shard_map/psum | solution.py:42
  133.2 9.2 %convolution_bitcast_fusion.1 = f32[1024,128]{0,1:T(8,128)} fusion(f32[2048,128]{1,0:T(8,128)} %all-reduce.7.cloned.1.call-done, f32[2048,1024]{1,0:T(8,128)} %param.5), kind=kOutput, calls=%fused_computation.1 | convolution fusion | flops 3221225472 | bytes 9961472 | tf_op jit(solution)/shard_map/dot_general | solution.py:43
  142.4 0.0 all-reduce.9.cloned.1.call-update
  142.4 0.2 reduce-scatter.2.cloned.1.call-start
  142.7 94.3 %all-reduce.9.cloned.1.call-done = f32[1024,128]{0,1:T(8,128)} async-done(((f32[1024,128]{0,1:T(8,128)}), f32[1024,128]{0,1:T(8,128)}) %all-reduce.9.cloned.1.call-update) | async-done | bytes 524304 | tf_op jit(solution)/shard_map/psum | solution.py:46
  236.9 13.0 %convolution_bitcast_fusion = f32[2048,128]{0,1:T(8,128)} fusion(f32[2048,1024]{1,0:T(8,128)} %param.5, f32[1024,128]{0,1:T(8,128)} %all-reduce.9.cloned.1.call-done), kind=kOutput, calls=%fused_computation | convolution fusion | flops 3221356544 | bytes 9961472 | tf_op jit(solution)/shard_map/dot_general | solution.py:48
  249.9 0.0 reduce-scatter.2.cloned.1.call-update
  249.9 0.0 all-reduce.11.cloned.1.call-start
  250.0 55.4 %reduce-scatter.2.cloned.1.call-done = f32[128,128]{0,1:T(8,128)} async-done(((f32[2048,128]{0,1:T(8,128)}), f32[128,128]{0,1:T(8,128)}) %reduce-scatter.2.cloned.1.call-update) | async-done | bytes 65552 | tf_op jit(solution)/shard_map/reduce_scatter | solution.py:47
  305.3 1.8 fusion.23
  307.1 0.0 all-reduce.11.cloned.1.call-update
  307.2 0.0 all-reduce.13.cloned.1.call-start
  307.2 101.7 %all-reduce.11.cloned.1.call-done = f32[128,128]{0,1:T(8,128)} async-done(((f32[128,128]{0,1:T(8,128)}), f32[128,128]{0,1:T(8,128)}) %all-reduce.11.cloned.1.call-update) | async-done | bytes 65552 | tf_op jit(solution)/shard_map/psum | solution.py:33
  408.9 0.0 all-reduce.13.cloned.1.call-update
  409.0 0.3 all-reduce.15.cloned.1.call-start
  409.2 90.4 %all-reduce.13.cloned.1.call-done = f32[128,128]{0,1:T(8,128)} async-done(((f32[128,128]{0,1:T(8,128)}), f32[128,128]{0,1:T(8,128)}) %all-reduce.13.cloned.1.call-update) | async-done | bytes 65552 | tf_op jit(solution)/shard_map/psum | solution.py:33
  499.6 0.9 copy.5
  500.6 0.9 fusion.6
  501.4 11.7 %cholesky.44 = f32[128,128]{1,0:T(8,128)S(1)} custom-call(f32[128,128]{1,0:T(8,128)S(1)} %fusion.6), custom_call_target="Cholesky" | custom-call | tf_op jit(solution)/shard_map/jit(cholesky)/cholesky | solution.py:18
  513.2 0.6 compare_reduce_fusion.1
  513.8 0.7 fusion.10
  514.5 9.8 %custom-call.6 = f32[1,128,128]{1,2,0:T(8,128)S(1)} custom-call(f32[1,128,128]{2,1,0:T(8,128)S(1)} %fusion.10), custom_call_target="InvertDiagBlocksLowerTriangular" | custom-call | tf_op jit(solution)/shard_map/triangular_solve/custom-call.0 | solution.py:19
  524.3 1.1 convolution_bitcast_fusion.3
  525.4 0.9 fusion.24
  526.3 0.0 all-reduce.15.cloned.1.call-update
  526.3 0.3 all-reduce.17.cloned.1.call-start
  526.6 100.1 %all-reduce.15.cloned.1.call-done = f32[128,128]{0,1:T(8,128)} async-done(((f32[128,128]{0,1:T(8,128)}), f32[128,128]{0,1:T(8,128)}) %all-reduce.15.cloned.1.call-update) | async-done | bytes 65552 | tf_op jit(solution)/shard_map/psum | solution.py:33
  626.8 0.0 all-reduce.17.cloned.1.call-update
  626.8 90.8 %all-reduce.17.cloned.1.call-done = f32[128,128]{0,1:T(8,128)} async-done(((f32[128,128]{0,1:T(8,128)}), f32[128,128]{0,1:T(8,128)}) %all-reduce.17.cloned.1.call-update) | async-done | bytes 65552 | tf_op jit(solution)/shard_map/psum | solution.py:33
  717.6 0.9 copy.7
  718.5 0.9 fusion.4
  719.4 11.7 %cholesky.55 = f32[128,128]{1,0:T(8,128)S(1)} custom-call(f32[128,128]{1,0:T(8,128)S(1)} %fusion.4), custom_call_target="Cholesky" | custom-call | tf_op jit(solution)/shard_map/jit(cholesky)/cholesky | solution.py:22
  731.1 0.7 compare_reduce_fusion
  731.8 2.3 convolution_multiply_fusion
  734.1 0.7 select_bitcast_fusion
  734.8 9.8 %custom-call.7 = f32[1,128,128]{1,2,0:T(8,128)S(1)} custom-call(f32[1,128,128]{2,1,0:T(8,128)S(1)} %select_bitcast_fusion), custom_call_target="InvertDiagBlocksLowerTriangular" | custom-call | tf_op jit(solution)/shard_map/triangular_solve/custom-call.0 | solution.py:23
  744.6 0.3 fusion
  744.9 0.7 copy.8
  (2 shorter events, 0.1 us)
Async XLA Ops:
  7.2 1.0 copy-start
  7.2 126.1 %all-reduce.7.cloned.1.call-start = ((), (), s32[]{:S(2)}) async-start(), calls=%async_computation.1 | async-start | bytes 2097152 | tf_op jit(solution)/shard_map/psum | solution.py:42
  18.1 218.8 %all-reduce.9.cloned.1.call-start = ((), (), s32[]{:S(2)}) async-start(), calls=%async_computation.2 | async-start | bytes 1048576 | tf_op jit(solution)/shard_map/psum | solution.py:46
  142.4 162.9 %reduce-scatter.2.cloned.1.call-start = ((), (), s32[]{:S(2)}) async-start(), calls=%async_computation.3 | async-start | bytes 1114112 | tf_op jit(solution)/shard_map/reduce_scatter | solution.py:47
  249.9 159.0 %all-reduce.11.cloned.1.call-start = ((), (), s32[]{:S(2)}) async-start(), calls=%async_computation.4 | async-start | bytes 131072 | tf_op jit(solution)/shard_map/psum | solution.py:33
  307.2 192.4 %all-reduce.13.cloned.1.call-start = ((), (), s32[]{:S(2)}) async-start(), calls=%async_computation.5 | async-start | bytes 131072 | tf_op jit(solution)/shard_map/psum | solution.py:33
  409.0 217.8 %all-reduce.15.cloned.1.call-start = ((), (), s32[]{:S(2)}) async-start(), calls=%async_computation.6 | async-start | bytes 131072 | tf_op jit(solution)/shard_map/psum | solution.py:33
  526.3 191.3 %all-reduce.17.cloned.1.call-start = ((), (), s32[]{:S(2)}) async-start(), calls=%async_computation.7 | async-start | bytes 131072 | tf_op jit(solution)/shard_map/psum | solution.py:33
Sparse Core Ops, SparseCore 0:
  18.2 114.9 all-reduce.6
  142.5 94.3 all-reduce.8
  250.1 55.2 reduce-scatter.1
  308.2 100.6 all-reduce.10
  412.0 87.5 all-reduce.12
  526.5 100.2 all-reduce.14
  630.0 87.5 all-reduce.16
